TPU v7x, 512 devices: a whole 4x4x16 slice. The times are simulated.
512 devices in a mesh: mp: 16 (over z), trow: 4 (over x), tcol: 8 (over y, core).
Axes of the slice: x: 4, y: 4, z: 16, core: 2. Of those that a mesh axis runs over, the one named last changes fastest.
Arguments:
- gram: float32 [16, 4096, 4096], P('mp', 'trow', 'tcol'), as said below
- rhs: float32 [256, 4096], P(('mp', 'tcol'), 'trow'), may hold values from -6 to 6
- guess: float32 [256, 4096], P(('mp', 'tcol'), 'trow'), may hold values from -6 to 6
Outputs:
- merged: float32 [256, 4096], P(('mp', 'tcol'), 'trow')
- residual: float32 [256, 4096], P(('mp', 'tcol'), 'trow')
Inputs may be any that keep to these rules, and one draw needn't show every extreme that they name: gram holds 16 symmetric positive definite matrices, one per model.
All inputs are finite; a program needn't handle non-finite values.
Results may differ from a plain program's by a relative error of at most 0.0003.
Values sent between devices are 32-bit elements; how exact they have to be, the bound alone decides.
No kernel may reach another device: no remote copies, remote signals or barrier semaphores. Data moves between devices by JAX's collectives and lax.ppermute only.
A program may use at most 64 MiB of HBM per device.

v0:
```python
import jax
import jax.numpy as jnp
from jax import lax
from jax.sharding import Mesh, PartitionSpec as P

MP = ("zk", "zb")
PLANE = ("trow", "tcol")
SHARD = ("trow", "zb")
HIGHEST = lax.Precision.HIGHEST


def dot(lhs, rhs, lhs_dim, rhs_dim):
    return lax.dot_general(
        lhs,
        rhs,
        (((lhs_dim,), (rhs_dim,)), ((), ())),
        precision=HIGHEST,
        preferred_element_type=jnp.float32,
    )


def exchange(pieces, axes):
    return lax.all_to_all(pieces, axes, 0, 0, tiled=True)


def spread(block, axes, count):
    return exchange(jnp.broadcast_to(block[None], (count,) + block.shape), axes)


def ordered(flag, mine, other):
    return (jnp.where(flag == 0, mine, other), jnp.where(flag == 0, other, mine))


def transposed(vector, sizes):
    trow, tcol = (sizes["trow"], sizes["tcol"])
    half = vector.shape[1] // 2
    core = lax.axis_index("tcol") % 2
    halves = (vector[:, :half], vector[:, half:])
    got = []
    for turn in range(2):
        pairs = []
        for i in range(trow):
            for j in range(tcol):
                q, h = (j // 2, j % 2)
                pairs.append((i * tcol + j, q * tcol + 2 * i + (h ^ turn)))
        sent = jnp.where(core == turn, halves[0], halves[1])
        got.append(lax.ppermute(sent, PLANE, pairs))
    return jnp.stack(ordered(core, got[0], got[1]))


def shards(sizes, gram, rhs, guess):
    zk, zb, trow, tcol = (sizes["zk"], sizes["zb"], sizes["trow"], sizes["tcol"])
    mp = zk * zb
    tile = gram[0]
    rows, cols = tile.shape
    own = rhs.shape[0]
    part_rows = rows // zb
    half = lax.axis_index("zb")
    cut = tile.reshape(zb, zk, part_rows // zk, cols).transpose(1, 0, 2, 3).reshape(rows, cols)
    part = lax.psum_scatter(cut, MP, scatter_dimension=0, tiled=True)
    total = lax.all_gather(part, "zk", axis=0, tiled=True)
    flipped = transposed(guess, sizes)
    over_mp = spread(flipped, MP, mp)
    over_mp = over_mp.transpose(1, 0, 2, 3).reshape(2 * mp * own, cols)
    block = spread(over_mp, "trow", trow).reshape(trow * 2 * mp * own, cols)
    terms = dot(block, tile, 1, 1)
    terms = exchange(terms.reshape(tcol, mp * own, rows), "tcol").sum(0)
    terms = exchange(terms.reshape(mp, own, rows), MP).sum(0)
    first = rhs - terms

    def halves(vector):
        low, high = (vector[:, :part_rows], vector[:, part_rows:])
        return (jnp.where(half == 0, low, high), jnp.where(half == 0, high, low))

    kept, given = halves(first)
    got = lax.ppermute(given, "zb", [(0, 1), (1, 0)])
    near = jnp.concatenate(ordered(half, kept, got))
    wide = spread(near, "tcol", tcol).reshape(tcol * zb * own, part_rows)
    second = spread(dot(wide, total, 1, 0), SHARD, trow * zb).sum(0)
    terms = dot(second, total, 1, 1)
    pieces = jnp.concatenate([terms, second], axis=1).reshape(tcol, zb * own, part_rows + cols)
    pieces = exchange(pieces, "tcol")
    third = pieces[:, :, :part_rows].sum(0)
    second = lax.dynamic_slice(
        pieces, (2 * lax.axis_index("trow"), 0, part_rows), (2, zb * own, cols)
    )
    second = jnp.concatenate([second[0], second[1]], axis=1)

    def inner(u, v):
        return jnp.sum(u * v, axis=1, keepdims=True)

    def inverse(x):
        return jnp.where(x > 0, 1.0 / jnp.where(x > 0, x, 1.0), 0.0)

    here, _ = halves(second)
    f0 = jnp.sqrt(inner(near, near))
    e0 = near * inverse(f0)
    s0 = inner(e0, here)
    rest = here - s0 * e0
    s1 = jnp.sqrt(inner(rest, rest))
    e1 = rest * inverse(s1)
    t0 = inner(e0, third)
    t1 = inner(e1, third - t0 * e0)
    known = jnp.concatenate(
        [third, jnp.pad(jnp.concatenate([f0, s0, s1, t0, t1], axis=1), ((0, 0), (0, 123)))], axis=1
    )
    wide_known = part_rows + 128
    pieces = jnp.broadcast_to(known[None], (trow,) + known.shape).reshape(
        trow * zb, own, wide_known
    )
    pieces = exchange(pieces, SHARD)
    f0, s0, s1, t0, t1 = (pieces[:, :, part_rows + n : part_rows + n + 1] for n in range(5))
    third = lax.dynamic_slice(pieces, (zb * lax.axis_index("trow"), 0, 0), (zb, own, part_rows))
    third = jnp.concatenate([third[0], third[1]], axis=1)
    second = jnp.where(half == 0, second[:own], second[own:])
    norm_first = jnp.sum(f0 * f0, 0)
    alpha = norm_first / jnp.sum(f0 * s0, 0)
    r0, r1 = (f0 - alpha * s0, -alpha * s1)
    norm_next = jnp.sum(r0 * r0 + r1 * r1, 0)
    beta = norm_next / norm_first
    d0, d1 = (r0 + beta * f0, r1)
    i0, i1 = (s0 - alpha * t0 + beta * s0, s1 - alpha * t1 + beta * s1)
    alpha_next = norm_next / jnp.sum(d0 * i0 + d1 * i1, 0)
    residual = first - alpha * second
    direction = residual + beta * first
    image = second - alpha * third + beta * second
    merged = guess + alpha * first + alpha_next * direction
    return (merged, residual - alpha_next * image)


def solution(mesh):
    mp, trow, tcol = (mesh.shape[a] for a in ("mp", "trow", "tcol"))
    sizes = {"zk": mp // 2, "zb": 2, "trow": trow, "tcol": tcol}
    split = Mesh(mesh.devices.reshape(tuple(sizes.values())), tuple(sizes))
    in_specs = (P(MP, "trow", "tcol"), P(MP + ("tcol",), "trow"), P(MP + ("tcol",), "trow"))
    out_specs = (P(MP + ("tcol",), "trow"), P(MP + ("tcol",), "trow"))

    def body(gram, rhs, guess):
        return shards(sizes, gram, rhs, guess)

    return jax.shard_map(body, mesh=split, in_specs=in_specs, out_specs=out_specs, check_vma=False)
```

profile of v0, /device:TPU:1, one launch (start us, length us, event | category | flops | bytes accessed | tf_op | source)
XLA Modules:
  0.0 193.3 jit_solution(9477022793621613023)
XLA Ops:
  7.2 0.0 reduce-scatter.2.cloned.1.call-start
  7.2 3.2 %copy.69 = f32[8,2,64,512]{3,2,1,0:T(8,128)} copy(f32[8,2,64,512]{3,2,0,1:T(8,128)} %bitcast.36) | data formatting | bytes 4194304 | tf_op jit(solution)/shard_map/transpose | solution.py:59
  10.4 0.0 copy-start.2
  10.4 0.0 copy-start
  10.4 0.0 reduce-scatter.2.cloned.1.call-update
  10.4 0.7 copy-done.2
  11.1 0.6 collective-permute-start
  11.7 8.8 %collective-permute-start.1 = (f32[2,512]{1,0:T(2,128)S(1)}, f32[2,512]{1,0:T(2,128)S(1)}, u32[]{:S(2)}, u32[]{:S(2)}) collective-permute-start(f32[2,512]{1,0:T(2,128)S(1)} %get-tuple-element.32), channel_id=1, source_target_pairs={{0,1},{1,0},{2,9},{3,8},{4,17},{5,16},{6,25},{7,24},{8,3},{9,2},{1... | collective-permute-start | bytes 12296 | tf_op jit(solution)/shard_map/ppermute | solution.py:47
  20.5 0.0 collective-permute-done
  20.6 0.8 collective-permute-done.1
  21.4 21.5 %all_to_all.40 = f32[16,2,2,512]{3,2,1,0:T(2,128)S(1)} all-to-all(f32[16,2,2,512]{3,2,1,0:T(2,128)S(1)} %broadcast_in_dim.23), channel_id=1, replica_groups=mesh['zk'=8,'zb'=2,'trow'=4,'tcol'=8] {'zk','zb'}, dimensions={0} | all-to-all | bytes 262144 | tf_op jit(solution)/shard_map/all_to_all | solution.py:23
  42.9 0.1 broadcast_in_dim.24
  43.0 0.1 broadcast_in_dim.25
  43.1 20.6 %all_to_all.41 = f32[4,64,512]{2,1,0:T(8,128)S(1)} all-to-all(f32[4,64,512]{2,1,0:T(8,128)S(1)} %broadcast_in_dim.25), channel_id=1, replica_groups=mesh['zk'=8,'zb'=2,'trow'=4,'tcol'=8] {'trow'}, dimensions={0} | all-to-all | bytes 1048576 | tf_op jit(solution)/shard_map/all_to_all | solution.py:23
  63.7 0.0 copy-done
  63.7 2.9 %fusion = f32[8,32,1024]{2,1,0:T(8,128)} fusion(f32[8,32,512]{2,1,0:T(8,128)S(1)} %bitcast.38, f32[1,1024,512]{2,1,0:T(8,128)S(1)} %copy-done), kind=kOutput, calls=%fused_computation | convolution fusion | flops 1610612736 | bytes 3670016 | tf_op jit(solution)/shard_map/dot_general | solution.py:13
  66.6 0.0 copy-start.3
  66.6 8.8 %all-to-all-start.2 = ((f32[8,32,1024]{2,1,0:T(8,128)}), f32[8,32,1024]{2,1,0:T(8,128)S(1)}, u32[]{:S(2)}, u32[]{:S(2)}) async-start(f32[8,32,1024]{2,1,0:T(8,128)} %fusion), calls=%async_computation.2 | async-start | bytes 2097152 | tf_op jit(solution)/shard_map/all_to_all | solution.py:23
  75.4 0.0 all-gather.2.cloned.1.call-start
  75.4 7.6 %reduce-scatter.2.cloned.1.call-done = f32[64,512]{1,0:T(8,128)} async-done(((f32[1024,512]{1,0:T(8,128)}), f32[64,512]{1,0:T(8,128)}) %reduce-scatter.2.cloned.1.call-update) | async-done | bytes 131088 | tf_op jit(solution)/shard_map/reduce_scatter | solution.py:60
  83.0 0.0 all-gather.2.cloned.1.call-update
  83.0 7.5 %all-to-all-done.2 = f32[8,32,1024]{2,1,0:T(8,128)S(1)} async-done(((f32[8,32,1024]{2,1,0:T(8,128)}), f32[8,32,1024]{2,1,0:T(8,128)S(1)}, u32[]{:S(2)}, u32[]{:S(2)}) %all-to-all-start.2) | async-done | bytes 1048608 | tf_op jit(solution)/shard_map/all_to_all | solution.py:23
  90.5 0.1 reduce_sum.117
  90.6 0.7 reshape.118
  91.3 5.5 %all-to-all-start.3 = ((f32[16,2,1024]{2,1,0:T(2,128)}), f32[16,2,1024]{2,1,0:T(2,128)S(1)}, u32[]{:S(2)}, u32[]{:S(2)}) async-start(f32[16,2,1024]{2,1,0:T(2,128)} %reshape.118), calls=%async_computation.3 | async-start | bytes 262144 | tf_op jit(solution)/shard_map/all_to_all | solution.py:23
  96.8 12.1 %all-to-all-done.3 = f32[16,2,1024]{2,1,0:T(2,128)S(1)} async-done(((f32[16,2,1024]{2,1,0:T(2,128)}), f32[16,2,1024]{2,1,0:T(2,128)S(1)}, u32[]{:S(2)}, u32[]{:S(2)}) %all-to-all-start.3) | async-done | bytes 131104 | tf_op jit(solution)/shard_map/all_to_all | solution.py:23
  108.8 0.1 reduce_sum.118
  108.9 0.0 copy-done.3
  108.9 2.8 %collective-permute-start.2 = (f32[2,512]{1,0:T(2,128)S(1)}, f32[2,512]{1,0:T(2,128)S(1)}, u32[]{:S(2)}, u32[]{:S(2)}) collective-permute-start(f32[2,512]{1,0:T(2,128)S(1)} %broadcast_select_fusion.5), channel_id=1, source_target_pairs={{0,32},{32,0},{1,33},{33,1},{2,34},{34,2},{3,35},{35,3},{4,36},{36... | collective-permute-start | bytes 12296 | tf_op jit(solution)/shard_map/ppermute | solution.py:76
  111.8 2.0 %collective-permute-done.2 = f32[2,512]{1,0:T(2,128)S(1)} collective-permute-done((f32[2,512]{1,0:T(2,128)S(1)}, f32[2,512]{1,0:T(2,128)S(1)}, u32[]{:S(2)}, u32[]{:S(2)}) %collective-permute-start.2) | collective-permute-done | bytes 4128 | tf_op jit(solution)/shard_map/ppermute | solution.py:76
  113.8 0.1 pad_maximum_fusion.3
  113.9 19.2 %all_to_all.42 = f32[8,4,512]{2,1,0:T(4,128)S(1)} all-to-all(f32[8,4,512]{2,1,0:T(4,128)S(1)} %broadcast_in_dim.26), channel_id=1, replica_groups=mesh['zk'=8,'zb'=2,'trow'=4,'tcol'=8] {'tcol'}, dimensions={0} | all-to-all | bytes 131072 | tf_op jit(solution)/shard_map/all_to_all | solution.py:23
  133.1 9.7 %all-gather.2.cloned.1.call-done = f32[512,512]{1,0:T(8,128)} async-done(((f32[64,512]{1,0:T(8,128)}), f32[512,512]{1,0:T(8,128)}) %all-gather.2.cloned.1.call-update) | async-done | bytes 1048592 | tf_op jit(solution)/shard_map/all_gather | solution.py:61
  142.8 0.0 copy-start.1
  142.8 2.0 %fusion.11 = f32[32,512]{1,0:T(8,128)S(1)} fusion(f32[32,512]{1,0:T(8,128)S(1)} %reshape.119, f32[512,512]{1,0:T(8,128)} %all-gather.2.cloned.1.call-done), kind=kOutput, calls=%fused_computation.52 | convolution fusion | flops 100663296 | bytes 1179648 | tf_op jit(solution)/shard_map/dot_general | solution.py:13
  144.8 0.9 broadcast_in_dim.27
  145.7 3.7 %all-to-all-start.5 = ((f32[8,32,512]{2,1,0:T(8,128)}), f32[8,32,512]{2,1,0:T(8,128)S(1)}, u32[]{:S(2)}, u32[]{:S(2)}) async-start(f32[8,32,512]{2,1,0:T(8,128)} %broadcast_in_dim.27), calls=%async_computation.6 | async-start | bytes 1048576 | tf_op jit(solution)/shard_map/all_to_all | solution.py:23
  149.4 7.5 %all-to-all-done.5 = f32[8,32,512]{2,1,0:T(8,128)S(1)} async-done(((f32[8,32,512]{2,1,0:T(8,128)}), f32[8,32,512]{2,1,0:T(8,128)S(1)}, u32[]{:S(2)}, u32[]{:S(2)}) %all-to-all-start.5) | async-done | bytes 524320 | tf_op jit(solution)/shard_map/all_to_all | solution.py:23
  157.0 0.0 copy-done.1
  157.0 1.0 fusion.12
  158.1 0.7 reshape.121
  158.7 11.2 %all-to-all-start.6 = ((f32[8,4,1024]{2,1,0:T(4,128)}), f32[8,4,1024]{2,1,0:T(4,128)S(1)}, u32[]{:S(2)}, u32[]{:S(2)}) async-start(f32[8,4,1024]{2,1,0:T(4,128)} %reshape.121), calls=%async_computation.7 | async-start | bytes 262144 | tf_op jit(solution)/shard_map/all_to_all | solution.py:23
  170.0 0.1 copy.70
  170.1 5.2 %all-to-all-done.6 = f32[8,4,1024]{2,1,0:T(4,128)S(1)} async-done(((f32[8,4,1024]{2,1,0:T(4,128)}), f32[8,4,1024]{2,1,0:T(4,128)S(1)}, u32[]{:S(2)}, u32[]{:S(2)}) %all-to-all-start.6) | async-done | bytes 131104 | tf_op jit(solution)/shard_map/all_to_all | solution.py:23
  175.3 0.2 multiply_reduce_fusion.3
  175.5 0.2 multiply_reduce_fusion.1
  175.7 0.2 multiply_reduce_fusion
  175.9 0.1 copy.74
  176.0 0.1 copy.72
  176.1 0.1 copy.73
  176.2 0.1 copy.71
  176.3 0.1 concatenate.20
  176.4 7.5 %all_to_all.43 = f32[8,2,640]{2,1,0:T(2,128)S(1)} all-to-all(f32[8,2,640]{2,1,0:T(2,128)S(1)} %reshape.122), channel_id=1, replica_groups=mesh['zk'=8,'zb'=2,'trow'=4,'tcol'=8] {'trow','zb'}, dimensions={0} | all-to-all | bytes 81920 | tf_op jit(solution)/shard_map/all_to_all | solution.py:23
  183.9 0.1 fusion.10
  184.0 0.1 copy.81
  184.1 0.1 copy.82
  184.2 0.1 copy.83
  184.3 0.2 multiply_reduce_fusion.5
  184.5 0.2 add_reduce_fusion.1
  184.7 0.1 copy.84
  184.8 0.1 copy.85
  184.9 0.2 add_reduce_fusion
  185.1 0.7 fusion.7
  185.8 0.7 multiply_add_fusion
  (22 shorter events, 0.3 us)
Async XLA Ops:
  7.2 75.9 %reduce-scatter.2.cloned.1.call-start = ((), (), s32[]{:S(2)}) async-start(), calls=%async_computation.9 | async-start | bytes 2228224 | tf_op jit(solution)/shard_map/reduce_scatter | solution.py:60
  10.4 0.7 copy-start.2
  10.4 53.3 %copy-start = (f32[1,1024,512]{2,1,0:T(8,128)S(1)}, f32[1,1024,512]{2,1,0:T(8,128)}, u32[]{:S(2)}) copy-start(f32[1,1024,512]{2,1,0:T(8,128)} %param.3) | copy-start | bytes 6291460
  11.1 9.5 %collective-permute-start = (f32[2,512]{1,0:T(2,128)S(1)}, f32[2,512]{1,0:T(2,128)S(1)}, u32[]{:S(2)}, u32[]{:S(2)}) collective-permute-start(f32[2,512]{1,0:T(2,128)S(1)} %get-tuple-element.31), channel_id=1, source_target_pairs={{0,0},{1,1},{2,8},{3,9},{4,16},{5,17},{6,24},{7,25},{8,2},{9,3},{1... | collective-permute-start | bytes 12296 | tf_op jit(solution)/shard_map/ppermute | solution.py:47
  11.7 9.6 %collective-permute-start.1 = (f32[2,512]{1,0:T(2,128)S(1)}, f32[2,512]{1,0:T(2,128)S(1)}, u32[]{:S(2)}, u32[]{:S(2)}) collective-permute-start(f32[2,512]{1,0:T(2,128)S(1)} %get-tuple-element.32), channel_id=1, source_target_pairs={{0,1},{1,0},{2,9},{3,8},{4,17},{5,16},{6,25},{7,24},{8,3},{9,2},{1... | collective-permute-start | bytes 12296 | tf_op jit(solution)/shard_map/ppermute | solution.py:47
  66.6 42.3 %copy-start.3 = (f32[2,1024]{1,0:T(2,128)S(1)}, f32[2,1024]{1,0:T(2,128)}, u32[]{:S(2)}) copy-start(f32[2,1024]{1,0:T(2,128)} %param.4) | copy-start | bytes 24580
  66.6 23.9 %all-to-all-start.2 = ((f32[8,32,1024]{2,1,0:T(8,128)}), f32[8,32,1024]{2,1,0:T(8,128)S(1)}, u32[]{:S(2)}, u32[]{:S(2)}) async-start(f32[8,32,1024]{2,1,0:T(8,128)} %fusion), calls=%async_computation.2 | async-start | bytes 2097152 | tf_op jit(solution)/shard_map/all_to_all | solution.py:23
  75.4 67.4 %all-gather.2.cloned.1.call-start = ((), (), s32[]{:S(2)}) async-start(), calls=%async_computation.10 | async-start | bytes 1179648 | tf_op jit(solution)/shard_map/all_gather | solution.py:61
  91.3 17.5 %all-to-all-start.3 = ((f32[16,2,1024]{2,1,0:T(2,128)}), f32[16,2,1024]{2,1,0:T(2,128)S(1)}, u32[]{:S(2)}, u32[]{:S(2)}) async-start(f32[16,2,1024]{2,1,0:T(2,128)} %reshape.118), calls=%async_computation.3 | async-start | bytes 262144 | tf_op jit(solution)/shard_map/all_to_all | solution.py:23
  108.9 4.8 %collective-permute-start.2 = (f32[2,512]{1,0:T(2,128)S(1)}, f32[2,512]{1,0:T(2,128)S(1)}, u32[]{:S(2)}, u32[]{:S(2)}) collective-permute-start(f32[2,512]{1,0:T(2,128)S(1)} %broadcast_select_fusion.5), channel_id=1, source_target_pairs={{0,32},{32,0},{1,33},{33,1},{2,34},{34,2},{3,35},{35,3},{4,36},{36... | collective-permute-start | bytes 12296 | tf_op jit(solution)/shard_map/ppermute | solution.py:76
  142.8 14.2 %copy-start.1 = (f32[512,512]{1,0:T(8,128)S(1)}, f32[512,512]{1,0:T(8,128)}, u32[]{:S(2)}) copy-start(f32[512,512]{1,0:T(8,128)} %all-gather.2.cloned.1.call-done) | copy-start | bytes 3145732
  145.7 11.2 %all-to-all-start.5 = ((f32[8,32,512]{2,1,0:T(8,128)}), f32[8,32,512]{2,1,0:T(8,128)S(1)}, u32[]{:S(2)}, u32[]{:S(2)}) async-start(f32[8,32,512]{2,1,0:T(8,128)} %broadcast_in_dim.27), calls=%async_computation.6 | async-start | bytes 1048576 | tf_op jit(solution)/shard_map/all_to_all | solution.py:23
  158.7 16.5 %all-to-all-start.6 = ((f32[8,4,1024]{2,1,0:T(4,128)}), f32[8,4,1024]{2,1,0:T(4,128)S(1)}, u32[]{:S(2)}, u32[]{:S(2)}) async-start(f32[8,4,1024]{2,1,0:T(4,128)} %reshape.121), calls=%async_computation.7 | async-start | bytes 262144 | tf_op jit(solution)/shard_map/all_to_all | solution.py:23
Sparse Core Ops, SparseCore 0:
  10.8 72.1 reduce-scatter.1
  85.1 57.6 all-gather.1
where the time goes:
time: 194 us; the launch traced here: 193 us
  blocking collectives  68.8 us (35%)
  waiting for transfers between devices  52.3 us (27%)
  starting transfers between devices  41.5 us (21%)
  between operations  14.3 us (7%)
  local copies, waits for them, and re-layouts  7.5 us (4%)
  matrix products  5.97 us (3%)
  other arithmetic  2.89 us (1%)
    all_to_all x4, blocking collectives, exchange(): return lax.all_to_all(pieces, axes, 0, 0, tiled=True)  68.8 us
    all_to_all x4, waiting for transfers between devices, exchange(): return lax.all_to_all(pieces, axes, 0, 0, tiled=True)  32.3 us
    all_to_all x4, starting transfers between devices, exchange(): return lax.all_to_all(pieces, axes, 0, 0, tiled=True)  29.1 us
    all_gather x1, waiting for transfers between devices, shards(): total = lax.all_gather(part, 'zk', axis=0, tiled=True)  9.67 us
    ppermute x2, starting transfers between devices, transposed(): got.append(lax.ppermute(sent, PLANE, pairs))  9.44 us
    reduce_scatter x1, waiting for transfers between devices, shards(): part = lax.psum_scatter(cut, MP, scatter_dimension=0, tiled=True)  7.61 us
    dot_general x3, matrix products, dot(): lax.dot_general(lhs, rhs, (((lhs_dim,), (rhs_dim,)), ((), ())), precision...  5.97 us
  transfers between devices with their start and end apart: 9, of which 8 were waited for; matrix products, arithmetic and copies ran while one was open for 2% of the time, Pallas kernels for 0%

commit v1 on v0

--- a/solution.py
+++ b/solution.py
@@ -58,7 +58,9 @@
     half = lax.axis_index("zb")
     cut = tile.reshape(zb, zk, part_rows // zk, cols).transpose(1, 0, 2, 3).reshape(rows, cols)
     part = lax.psum_scatter(cut, MP, scatter_dimension=0, tiled=True)
-    total = lax.all_gather(part, "zk", axis=0, tiled=True)
+    total = jnp.concatenate(
+        lax.all_to_all(jnp.stack([part] * lax.axis_size("zk")), "zk", 0, 0), axis=0
+    )
     flipped = transposed(guess, sizes)
     over_mp = spread(flipped, MP, mp)
     over_mp = over_mp.transpose(1, 0, 2, 3).reshape(2 * mp * own, cols)

time: 194 us -> 227 us (1.17)
  waiting for transfers between devices: 52.3 us -> 68 us
  blocking collectives: 68.8 us -> 84.3 us
  starting transfers between devices: 41.5 us -> 43.8 us
  matrix products: 5.97 us -> 3.68 us
    all_to_all x0 -> x1, waiting for transfers between devices: none -> 41.1 us  [shards(): lax.all_to_all(jnp.stack([part] * lax.axis_size('zk')), 'zk', 0, 0)]
    all_to_all x4 -> x5, blocking collectives: 68.8 us -> 84.3 us  [exchange(): return lax.all_to_all(pieces, axes, 0, 0, tiled=True)]
    all_gather x1 -> x0, waiting for transfers between devices: 9.67 us -> none  [shards(): total = lax.all_gather(part, 'zk', axis=0, tiled=True)]
    reduce_scatter x1, waiting for transfers between devices: 7.61 us -> 0.01 us  [shards(): part = lax.psum_scatter(cut, MP, scatter_dimension=0, tiled=True)]
    all_to_all x4 -> x3, waiting for transfers between devices: 32.3 us -> 24.7 us  [exchange(): return lax.all_to_all(pieces, axes, 0, 0, tiled=True)]
    all_to_all x0 -> x1, starting transfers between devices: none -> 3.6 us  [shards(): lax.all_to_all(jnp.stack([part] * lax.axis_size('zk')), 'zk', 0, 0)]
    dot_general x3, matrix products: 5.97 us -> 3.68 us  [dot(): lax.dot_general(lhs, rhs, (((lhs_dim,), (rhs_dim,)), ((), ())), precision...]
    all_to_all x4 -> x3, starting transfers between devices: 29.1 us -> 27.7 us  [exchange(): return lax.all_to_all(pieces, axes, 0, 0, tiled=True)]
  transfers between devices with their start and end apart: 9 -> 8, of which waited for: 8 -> 6; matrix products, arithmetic and copies ran while one was open for 2% -> 1% of each run, Pallas kernels for 0% -> 0%
where the time goes in v1:
time: 227 us; the launch traced here: 226 us
  blocking collectives  84.3 us (37%)
  waiting for transfers between devices  68 us (30%)
  starting transfers between devices  43.8 us (19%)
  between operations  14.3 us (6%)
  local copies, waits for them, and re-layouts  9.49 us (4%)
  matrix products  3.68 us (2%)
  other arithmetic  2.89 us (1%)
    all_to_all x5, blocking collectives, exchange(): return lax.all_to_all(pieces, axes, 0, 0, tiled=True)  84.3 us
    all_to_all x1, waiting for transfers between devices, shards(): lax.all_to_all(jnp.stack([part] * lax.axis_size('zk')), 'zk', 0, 0)  41.1 us
    all_to_all x3, starting transfers between devices, exchange(): return lax.all_to_all(pieces, axes, 0, 0, tiled=True)  27.7 us
    all_to_all x3, waiting for transfers between devices, exchange(): return lax.all_to_all(pieces, axes, 0, 0, tiled=True)  24.7 us
    ppermute x2, starting transfers between devices, transposed(): got.append(lax.ppermute(sent, PLANE, pairs))  9.44 us
  transfers between devices with their start and end apart: 8, of which 6 were waited for; matrix products, arithmetic and copies ran while one was open for 1% of the time, Pallas kernels for 0%

profile of v1, /device:TPU:1, one launch (start us, length us, event | category | flops | bytes accessed | tf_op | source)
XLA Modules:
  0.0 226.4 jit_solution(85106017506046296)
XLA Ops:
  7.2 0.0 reduce-scatter.2.cloned.1.call-start
  7.2 3.2 %copy.69 = f32[8,2,64,512]{3,2,1,0:T(8,128)} copy(f32[8,2,64,512]{3,2,0,1:T(8,128)} %bitcast.39) | data formatting | bytes 4194304 | tf_op jit(solution)/shard_map/transpose | solution.py:59
  10.4 0.0 copy-start.1
  10.4 0.0 copy-start
  10.4 0.0 reduce-scatter.2.cloned.1.call-update
  10.4 0.7 copy-done.1
  11.1 0.6 collective-permute-start
  11.7 8.8 %collective-permute-start.1 = (f32[2,512]{1,0:T(2,128)S(1)}, f32[2,512]{1,0:T(2,128)S(1)}, u32[]{:S(2)}, u32[]{:S(2)}) collective-permute-start(f32[2,512]{1,0:T(2,128)S(1)} %get-tuple-element.32), channel_id=1, source_target_pairs={{0,1},{1,0},{2,9},{3,8},{4,17},{5,16},{6,25},{7,24},{8,3},{9,2},{1... | collective-permute-start | bytes 12296 | tf_op jit(solution)/shard_map/ppermute | solution.py:47
  20.5 0.0 collective-permute-done
  20.6 0.8 collective-permute-done.1
  21.4 21.5 %all_to_all.45 = f32[16,2,2,512]{3,2,1,0:T(2,128)S(1)} all-to-all(f32[16,2,2,512]{3,2,1,0:T(2,128)S(1)} %broadcast_in_dim.23), channel_id=1, replica_groups=mesh['zk'=8,'zb'=2,'trow'=4,'tcol'=8] {'zk','zb'}, dimensions={0} | all-to-all | bytes 262144 | tf_op jit(solution)/shard_map/all_to_all | solution.py:23
  42.9 0.1 broadcast_in_dim.24
  43.0 0.1 broadcast_in_dim.25
  43.1 20.6 %all_to_all.46 = f32[4,64,512]{2,1,0:T(8,128)S(1)} all-to-all(f32[4,64,512]{2,1,0:T(8,128)S(1)} %broadcast_in_dim.25), channel_id=1, replica_groups=mesh['zk'=8,'zb'=2,'trow'=4,'tcol'=8] {'trow'}, dimensions={0} | all-to-all | bytes 1048576 | tf_op jit(solution)/shard_map/all_to_all | solution.py:23
  63.7 0.0 copy-done
  63.7 1.9 fusion
  65.6 0.0 copy-start.2
  65.7 22.8 %all_to_all.47 = f32[8,32,1024]{2,1,0:T(8,128)S(1)} all-to-all(f32[8,32,1024]{2,1,0:T(8,128)S(1)} %fusion), channel_id=1, replica_groups=mesh['zk'=8,'zb'=2,'trow'=4,'tcol'=8] {'tcol'}, dimensions={0} | all-to-all | bytes 2097152 | tf_op jit(solution)/shard_map/all_to_all | solution.py:23
  88.4 0.1 reduce_sum.117
  88.5 0.7 reshape.123
  89.2 5.5 %all-to-all-start.3 = ((f32[16,2,1024]{2,1,0:T(2,128)}), f32[16,2,1024]{2,1,0:T(2,128)S(1)}, u32[]{:S(2)}, u32[]{:S(2)}) async-start(f32[16,2,1024]{2,1,0:T(2,128)} %reshape.123), calls=%async_computation.3 | async-start | bytes 262144 | tf_op jit(solution)/shard_map/all_to_all | solution.py:23
  94.7 12.0 %all-to-all-done.3 = f32[16,2,1024]{2,1,0:T(2,128)S(1)} async-done(((f32[16,2,1024]{2,1,0:T(2,128)}), f32[16,2,1024]{2,1,0:T(2,128)S(1)}, u32[]{:S(2)}, u32[]{:S(2)}) %all-to-all-start.3) | async-done | bytes 131104 | tf_op jit(solution)/shard_map/all_to_all | solution.py:23
  106.7 0.1 reduce_sum.118
  106.7 0.0 copy-done.2
  106.8 3.0 %collective-permute-start.2 = (f32[2,512]{1,0:T(2,128)S(1)}, f32[2,512]{1,0:T(2,128)S(1)}, u32[]{:S(2)}, u32[]{:S(2)}) collective-permute-start(f32[2,512]{1,0:T(2,128)S(1)} %broadcast_select_fusion.5), channel_id=1, source_target_pairs={{0,32},{32,0},{1,33},{33,1},{2,34},{34,2},{3,35},{35,3},{4,36},{36... | collective-permute-start | bytes 12296 | tf_op jit(solution)/shard_map/ppermute | solution.py:78
  109.7 1.4 collective-permute-done.2
  111.1 0.1 pad_maximum_fusion.3
  111.3 11.9 %all_to_all.48 = f32[8,4,512]{2,1,0:T(4,128)S(1)} all-to-all(f32[8,4,512]{2,1,0:T(4,128)S(1)} %broadcast_in_dim.26), channel_id=1, replica_groups=mesh['zk'=8,'zb'=2,'trow'=4,'tcol'=8] {'tcol'}, dimensions={0} | all-to-all | bytes 131072 | tf_op jit(solution)/shard_map/all_to_all | solution.py:23
  123.2 0.0 reduce-scatter.2.cloned.1.call-done
  123.2 2.0 stack.11
  125.2 3.6 %all-to-all-start.5 = ((f32[8,64,512]{2,1,0:T(8,128)}), f32[8,64,512]{2,1,0:T(8,128)S(1)}, u32[]{:S(2)}, u32[]{:S(2)}) async-start(f32[8,64,512]{2,1,0:T(8,128)} %stack.11), calls=%async_computation.6 | async-start | bytes 2097152 | tf_op jit(solution)/shard_map/all_to_all | solution.py:62
  128.8 41.1 %all-to-all-done.5 = f32[8,64,512]{2,1,0:T(8,128)S(1)} async-done(((f32[8,64,512]{2,1,0:T(8,128)}), f32[8,64,512]{2,1,0:T(8,128)S(1)}, u32[]{:S(2)}, u32[]{:S(2)}) %all-to-all-start.5) | async-done | bytes 1048608 | tf_op jit(solution)/shard_map/all_to_all | solution.py:62
  169.9 0.7 fusion.11
  170.6 0.8 broadcast_in_dim.27
  171.4 11.7 %all-to-all-start.6 = ((f32[8,32,512]{2,1,0:T(8,128)}), f32[8,32,512]{2,1,0:T(8,128)S(1)}, u32[]{:S(2)}, u32[]{:S(2)}) async-start(f32[8,32,512]{2,1,0:T(8,128)} %broadcast_in_dim.27), calls=%async_computation.7 | async-start | bytes 1048576 | tf_op jit(solution)/shard_map/all_to_all | solution.py:23
  183.2 7.5 %all-to-all-done.6 = f32[8,32,512]{2,1,0:T(8,128)S(1)} async-done(((f32[8,32,512]{2,1,0:T(8,128)}), f32[8,32,512]{2,1,0:T(8,128)S(1)}, u32[]{:S(2)}, u32[]{:S(2)}) %all-to-all-start.6) | async-done | bytes 524320 | tf_op jit(solution)/shard_map/all_to_all | solution.py:23
  190.7 1.0 fusion.12
  191.8 0.7 reshape.127
  192.5 10.5 %all-to-all-start.7 = ((f32[8,4,1024]{2,1,0:T(4,128)}), f32[8,4,1024]{2,1,0:T(4,128)S(1)}, u32[]{:S(2)}, u32[]{:S(2)}) async-start(f32[8,4,1024]{2,1,0:T(4,128)} %reshape.127), calls=%async_computation.8 | async-start | bytes 262144 | tf_op jit(solution)/shard_map/all_to_all | solution.py:23
  203.1 0.1 copy.70
  203.1 5.2 %all-to-all-done.7 = f32[8,4,1024]{2,1,0:T(4,128)S(1)} async-done(((f32[8,4,1024]{2,1,0:T(4,128)}), f32[8,4,1024]{2,1,0:T(4,128)S(1)}, u32[]{:S(2)}, u32[]{:S(2)}) %all-to-all-start.7) | async-done | bytes 131104 | tf_op jit(solution)/shard_map/all_to_all | solution.py:23
  208.4 0.2 multiply_reduce_fusion.3
  208.5 0.2 multiply_reduce_fusion.1
  208.8 0.2 multiply_reduce_fusion
  209.0 0.1 copy.74
  209.1 0.1 copy.72
  209.2 0.1 copy.73
  209.3 0.1 copy.71
  209.4 0.1 concatenate.20
  209.5 7.5 %all_to_all.49 = f32[8,2,640]{2,1,0:T(2,128)S(1)} all-to-all(f32[8,2,640]{2,1,0:T(2,128)S(1)} %reshape.128), channel_id=1, replica_groups=mesh['zk'=8,'zb'=2,'trow'=4,'tcol'=8] {'trow','zb'}, dimensions={0} | all-to-all | bytes 81920 | tf_op jit(solution)/shard_map/all_to_all | solution.py:23
  217.0 0.1 fusion.10
  217.1 0.1 copy.81
  217.2 0.1 copy.82
  217.3 0.1 copy.83
  217.4 0.2 multiply_reduce_fusion.5
  217.6 0.2 add_reduce_fusion.1
  217.8 0.1 copy.84
  217.9 0.1 copy.85
  217.9 0.2 add_reduce_fusion
  218.2 0.7 fusion.7
  218.9 0.7 multiply_add_fusion
  (22 shorter events, 0.3 us)
Async XLA Ops:
  7.2 116.0 %reduce-scatter.2.cloned.1.call-start = ((), (), s32[]{:S(2)}) async-start(), calls=%async_computation.10 | async-start | bytes 2228224 | tf_op jit(solution)/shard_map/reduce_scatter | solution.py:60
  10.4 0.7 copy-start.1
  10.4 53.3 %copy-start = (f32[1,1024,512]{2,1,0:T(8,128)S(1)}, f32[1,1024,512]{2,1,0:T(8,128)}, u32[]{:S(2)}) copy-start(f32[1,1024,512]{2,1,0:T(8,128)} %param.3) | copy-start | bytes 6291460
  11.1 9.5 %collective-permute-start = (f32[2,512]{1,0:T(2,128)S(1)}, f32[2,512]{1,0:T(2,128)S(1)}, u32[]{:S(2)}, u32[]{:S(2)}) collective-permute-start(f32[2,512]{1,0:T(2,128)S(1)} %get-tuple-element.31), channel_id=1, source_target_pairs={{0,0},{1,1},{2,8},{3,9},{4,16},{5,17},{6,24},{7,25},{8,2},{9,3},{1... | collective-permute-start | bytes 12296 | tf_op jit(solution)/shard_map/ppermute | solution.py:47
  11.7 9.6 %collective-permute-start.1 = (f32[2,512]{1,0:T(2,128)S(1)}, f32[2,512]{1,0:T(2,128)S(1)}, u32[]{:S(2)}, u32[]{:S(2)}) collective-permute-start(f32[2,512]{1,0:T(2,128)S(1)} %get-tuple-element.32), channel_id=1, source_target_pairs={{0,1},{1,0},{2,9},{3,8},{4,17},{5,16},{6,25},{7,24},{8,3},{9,2},{1... | collective-permute-start | bytes 12296 | tf_op jit(solution)/shard_map/ppermute | solution.py:47
  65.6 41.1 %copy-start.2 = (f32[2,1024]{1,0:T(2,128)S(1)}, f32[2,1024]{1,0:T(2,128)}, u32[]{:S(2)}) copy-start(f32[2,1024]{1,0:T(2,128)} %param.4) | copy-start | bytes 24580
  89.2 17.5 %all-to-all-start.3 = ((f32[16,2,1024]{2,1,0:T(2,128)}), f32[16,2,1024]{2,1,0:T(2,128)S(1)}, u32[]{:S(2)}, u32[]{:S(2)}) async-start(f32[16,2,1024]{2,1,0:T(2,128)} %reshape.123), calls=%async_computation.3 | async-start | bytes 262144 | tf_op jit(solution)/shard_map/all_to_all | solution.py:23
  106.8 4.4 %collective-permute-start.2 = (f32[2,512]{1,0:T(2,128)S(1)}, f32[2,512]{1,0:T(2,128)S(1)}, u32[]{:S(2)}, u32[]{:S(2)}) collective-permute-start(f32[2,512]{1,0:T(2,128)S(1)} %broadcast_select_fusion.5), channel_id=1, source_target_pairs={{0,32},{32,0},{1,33},{33,1},{2,34},{34,2},{3,35},{35,3},{4,36},{36... | collective-permute-start | bytes 12296 | tf_op jit(solution)/shard_map/ppermute | solution.py:78
  125.2 44.7 %all-to-all-start.5 = ((f32[8,64,512]{2,1,0:T(8,128)}), f32[8,64,512]{2,1,0:T(8,128)S(1)}, u32[]{:S(2)}, u32[]{:S(2)}) async-start(f32[8,64,512]{2,1,0:T(8,128)} %stack.11), calls=%async_computation.6 | async-start | bytes 2097152 | tf_op jit(solution)/shard_map/all_to_all | solution.py:62
  171.4 19.3 %all-to-all-start.6 = ((f32[8,32,512]{2,1,0:T(8,128)}), f32[8,32,512]{2,1,0:T(8,128)S(1)}, u32[]{:S(2)}, u32[]{:S(2)}) async-start(f32[8,32,512]{2,1,0:T(8,128)} %broadcast_in_dim.27), calls=%async_computation.7 | async-start | bytes 1048576 | tf_op jit(solution)/shard_map/all_to_all | solution.py:23
  192.5 15.8 %all-to-all-start.7 = ((f32[8,4,1024]{2,1,0:T(4,128)}), f32[8,4,1024]{2,1,0:T(4,128)S(1)}, u32[]{:S(2)}, u32[]{:S(2)}) async-start(f32[8,4,1024]{2,1,0:T(4,128)} %reshape.127), calls=%async_computation.8 | async-start | bytes 262144 | tf_op jit(solution)/shard_map/all_to_all | solution.py:23
Sparse Core Ops, SparseCore 0:
  10.8 72.3 reduce-scatter.1
